TPU v7x, 256 devices: a whole 4x4x8 slice. The times are simulated.
256 devices in a mesh: dp: 8 (over x, core), seq: 32 (over z, y).
Axes of the slice: x: 4, y: 4, z: 8, core: 2. Of those that a mesh axis runs over, the one named last changes fastest.
Arguments:
- queries: bfloat16 [49152, 512], P(('dp', 'seq')), may hold values from -6 to 6
- key_vectors: bfloat16 [49152, 512], P(('dp', 'seq')), may hold values from -6 to 6
- value_vectors: bfloat16 [49152, 512], P(('dp', 'seq')), may hold values from -6 to 6
- gate_values: bfloat16 [49152, 512], P(('dp', 'seq')), may hold values from -6 to 6
- norm_gain: float32 [512], replicated, may hold values from 0.5 to 2
- out_weight: bfloat16 [512, 1024], replicated, may hold values from -0.25 to 0.25
- out_grad: bfloat16 [49152, 1024], P(('dp', 'seq')), may hold values from -6 to 6
- history_lengths: int32 [8, 4], P('dp'), may hold values from 1 to 6048, 6144 in all within a row
Outputs:
- layer_out: bfloat16 [49152, 1024], P(('dp', 'seq'))
- query_grad: bfloat16 [49152, 512], P(('dp', 'seq'))
- key_grad: bfloat16 [49152, 512], P(('dp', 'seq'))
- value_grad: bfloat16 [49152, 512], P(('dp', 'seq'))
- gate_grad: bfloat16 [49152, 512], P(('dp', 'seq'))
- weight_grad: float32 [512, 1024], P('seq')
Inputs may be any that keep to these rules, and one draw needn't show every extreme that they name: `history_lengths`: in every row the 4 lengths sum to 6144, and the largest of them is exactly 6048.
All inputs are finite; a program needn't handle non-finite values.
Results may differ from a plain program's by a relative error of at most 0.015.
Values may be sent and summed in bfloat16 or wider, within the bound.
A program may use at most 128 MiB of HBM per device.

v0:
```python
import math

import jax
import jax.numpy as jnp
from jax import lax
from jax.sharding import PartitionSpec as P

HEAD = 128


NORM_EPSILON = 1e-05


def history_of(history_ends, places):
    return jnp.sum((places[:, None] >= history_ends[None, :]).astype(jnp.int32), axis=1)


def score_block(query_heads, query_places, key_heads, key_places, history_ends):
    scores = jnp.einsum(
        "qhd,khd->hqk", query_heads, key_heads, preferred_element_type=jnp.float32
    ) * HEAD ** (-0.5)
    same_owner = (
        history_of(history_ends, query_places)[:, None]
        == history_of(history_ends, key_places)[None, :]
    )
    visible = (same_owner & (query_places[:, None] >= key_places[None, :])).astype(jnp.float32)
    gates = jax.nn.sigmoid(scores)
    return (scores, gates, visible)


def grad_terms(
    query_heads, grad_heads, query_places, key_heads, value_heads, key_places, history_ends
):
    scores, gates, visible = score_block(
        query_heads, query_places, key_heads, key_places, history_ends
    )
    weights = (scores * gates * visible).astype(jnp.bfloat16)
    grad_weights = jnp.einsum(
        "qhd,khd->hqk", grad_heads, value_heads, preferred_element_type=jnp.float32
    )
    grad_scores = (grad_weights * gates * (1.0 + scores * (1.0 - gates)) * visible).astype(
        jnp.bfloat16
    )
    return (weights, grad_scores)


def per_device(
    queries,
    key_vectors,
    value_vectors,
    gate_values,
    norm_gain,
    out_weight,
    out_grad,
    history_lengths,
):
    local_rows, feature_width = queries.shape
    head_count = feature_width // HEAD
    group_size = lax.axis_size("seq")
    history_span = local_rows * group_size
    key_block = min(512, history_span)
    block_count = history_span // key_block
    score_scale = HEAD ** (-0.5)
    first_row = lax.axis_index("seq") * local_rows
    history_ends = jnp.cumsum(history_lengths[0])
    own_places = first_row + jnp.arange(local_rows, dtype=jnp.int32)
    query_heads = queries.reshape(local_rows, head_count, HEAD)
    keys_all, values_all = (
        lax.all_gather(key_vectors, "seq", axis=0, tiled=True),
        lax.all_gather(value_vectors, "seq", axis=0, tiled=True),
    )

    def block_of(block_index):
        start_row = block_index * key_block
        key_heads = lax.dynamic_slice_in_dim(keys_all, start_row, key_block, 0).reshape(
            key_block, head_count, HEAD
        )
        value_heads = lax.dynamic_slice_in_dim(values_all, start_row, key_block, 0).reshape(
            key_block, head_count, HEAD
        )
        key_places = start_row + jnp.arange(key_block, dtype=jnp.int32)
        return (key_heads, value_heads, key_places)

    def forward_step(block_index, attention):
        key_heads, value_heads, key_places = block_of(block_index)
        scores, gates, visible = score_block(
            query_heads, own_places, key_heads, key_places, history_ends
        )
        weights = (scores * gates * visible).astype(jnp.bfloat16)
        return attention + jnp.einsum(
            "hqk,khd->qhd", weights, value_heads, preferred_element_type=jnp.float32
        )

    zero_heads = jnp.zeros((local_rows, head_count, HEAD), jnp.float32)
    attention = lax.fori_loop(0, block_count, forward_step, zero_heads).reshape(
        local_rows, feature_width
    )
    row_mean = jnp.mean(attention, axis=1, keepdims=True)
    centred = attention - row_mean
    inv_std = 1.0 / jnp.sqrt(jnp.mean(centred * centred, axis=1, keepdims=True) + NORM_EPSILON)
    unit_attn = centred * inv_std
    normed = unit_attn * norm_gain
    gated_out = (normed * gate_values.astype(jnp.float32)).astype(jnp.bfloat16)
    layer_out = jnp.dot(gated_out, out_weight, preferred_element_type=jnp.float32).astype(
        jnp.bfloat16
    )
    grad_gated = jnp.einsum("te,ce->tc", out_grad, out_weight, preferred_element_type=jnp.float32)
    gate_grad = (grad_gated * normed).astype(jnp.bfloat16)
    grad_hat = grad_gated * gate_values.astype(jnp.float32) * norm_gain
    grad_mean = jnp.mean(grad_hat, axis=1, keepdims=True)
    grad_proj = jnp.mean(grad_hat * unit_attn, axis=1, keepdims=True)
    attn_grad = (inv_std * (grad_hat - grad_mean - unit_attn * grad_proj)).astype(jnp.bfloat16)
    grad_heads = attn_grad.reshape(local_rows, head_count, HEAD)

    def backward_step(block_index, carried):
        query_total, score_buffer, weight_buffer = carried
        key_heads, value_heads, key_places = block_of(block_index)
        weights, grad_scores = grad_terms(
            query_heads, grad_heads, own_places, key_heads, value_heads, key_places, history_ends
        )
        query_total = (
            query_total
            + jnp.einsum("hqk,khd->qhd", grad_scores, key_heads, preferred_element_type=jnp.float32)
            * score_scale
        )
        return (query_total, score_buffer, weight_buffer)

    empty_buffer = jnp.zeros((1,), jnp.bfloat16)
    query_total, score_buffer, weight_buffer = lax.fori_loop(
        0, block_count, backward_step, (zero_heads, empty_buffer, empty_buffer)
    )
    query_grad = query_total.reshape(local_rows, feature_width).astype(jnp.bfloat16)
    own_keys = key_vectors.reshape(local_rows, head_count, HEAD)
    own_values = value_vectors.reshape(local_rows, head_count, HEAD)
    query_piece = lax.all_gather(queries, "seq", axis=0, tiled=True)
    grad_piece = lax.all_gather(attn_grad, "seq", axis=0, tiled=True)
    row_count = query_piece.shape[0]
    sub_rows = math.gcd(row_count, 512)

    def inner(sub_index, running):
        offset = sub_index * sub_rows
        piece_heads = lax.dynamic_slice_in_dim(query_piece, offset, sub_rows, 0).reshape(
            sub_rows, head_count, HEAD
        )
        piece_grads = lax.dynamic_slice_in_dim(grad_piece, offset, sub_rows, 0).reshape(
            sub_rows, head_count, HEAD
        )
        piece_places = offset + jnp.arange(sub_rows, dtype=jnp.int32)
        key_total, value_total = running
        weights, grad_scores = grad_terms(
            piece_heads, piece_grads, piece_places, own_keys, own_values, own_places, history_ends
        )
        key_total = (
            key_total
            + jnp.einsum(
                "hqk,qhd->khd", grad_scores, piece_heads, preferred_element_type=jnp.float32
            )
            * score_scale
        )
        value_total = value_total + jnp.einsum(
            "hqk,qhd->khd", weights, piece_grads, preferred_element_type=jnp.float32
        )
        return (key_total, value_total)

    key_total, value_total = lax.fori_loop(
        0, row_count // sub_rows, inner, (zero_heads, zero_heads)
    )
    key_grad = key_total.reshape(local_rows, feature_width).astype(jnp.bfloat16)
    value_grad = value_total.reshape(local_rows, feature_width).astype(jnp.bfloat16)
    all_rows = history_span * lax.axis_size("dp")
    factor = all_rows ** (-0.5)
    share_rows = feature_width // group_size
    full_term = jnp.einsum("tc,te->ce", gated_out, out_grad, preferred_element_type=jnp.float32)
    summed = lax.psum(full_term, ("dp", "seq"))
    weight_grad = (
        lax.dynamic_slice_in_dim(summed, lax.axis_index("seq") * share_rows, share_rows, 0) * factor
    )
    return (layer_out, query_grad, key_grad, value_grad, gate_grad, weight_grad)


def solution(mesh):
    placed = (
        P(("dp", "seq"), None),
        P(("dp", "seq"), None),
        P(("dp", "seq"), None),
        P(("dp", "seq"), None),
        P(),
        P(),
        P(("dp", "seq"), None),
        P("dp", None),
    )
    return jax.shard_map(
        per_device,
        mesh=mesh,
        in_specs=placed,
        out_specs=(
            P(("dp", "seq"), None),
            P(("dp", "seq"), None),
            P(("dp", "seq"), None),
            P(("dp", "seq"), None),
            P(("dp", "seq"), None),
            P("seq", None),
        ),
        check_vma=False,
    )
```

profile of v0, /device:TPU:1, one launch (start us, length us, event | category | flops | bytes accessed | tf_op | source)
XLA Modules:
  0.0 827.4 jit_solution(6756446624285700892)
XLA Ops:
  11.2 91.6 %all-gather.5.cloned.1.call-done = bf16[6144,512]{1,0:T(8,128)(2,1)} async-done(((bf16[192,512]{1,0:T(8,128)(2,1)}), bf16[6144,512]{1,0:T(8,128)(2,1)}) %all-gather.5.cloned.1.call-update) | async-done | bytes 6291472 | tf_op jit(solution)/shard_map/all_gather | solution.py:70
  102.8 8.7 %copy.113 = bf16[6144,512]{0,1:T(8,128)(2,1)} copy(bf16[6144,512]{1,0:T(8,128)(2,1)} %all-gather.5.cloned.1.call-done) | data formatting | bytes 12582912
  111.5 79.6 %all-gather.7.cloned.1.call-done = bf16[6144,512]{1,0:T(8,128)(2,1)} async-done(((bf16[192,512]{1,0:T(8,128)(2,1)}), bf16[6144,512]{1,0:T(8,128)(2,1)}) %all-gather.7.cloned.1.call-update) | async-done | bytes 6291472 | tf_op jit(solution)/shard_map/all_gather | solution.py:69
  191.1 8.7 %copy.114 = bf16[6144,512]{0,1:T(8,128)(2,1)} copy(bf16[6144,512]{1,0:T(8,128)(2,1)} %all-gather.7.cloned.1.call-done) | data formatting | bytes 12582912
  199.7 41.7 %while.44 = (s32[]{:T(128)}, f32[192,4,128]{2,0,1:T(8,128)S(1)}, bf16[6144,512]{0,1:T(8,128)(2,1)}, bf16[6144,512]{0,1:T(8,128)(2,1)}, bf16[192,4,128]{2,0,1:T(8...) while((s32[]{:T(128)}, f32[192,4,128]{2,0,1:T(8,128)S(1)}, ...), condition=%wide.region_4.5_spmd.clone, body=%wide.region_1.4_spmd.clone.sunk | while | flops 204677376 | bytes 4929497 | solution.py:95
  248.3 80.3 %while.45 = (s32[]{:T(128)}, f32[192,4,128]{2,0,1:T(8,128)}, bf16[6144,512]{0,1:T(8,128)(2,1)}, bf16[6144,512]{0,1:T(8,128)(2,1)}, bf16[192,4,128]{2,0,1:T(8,128...) while((s32[]{:T(128)}, f32[192,4,128]{2,0,1:T(8,128)}, ...), condition=%wide.region_12.13_spmd.clone, body=%wide.region_9.12_spmd.clone.sunk | while | flops 307011840 | bytes 8796129 | solution.py:129
  252.0 2.9 fusion.105
  258.6 3.0 fusion.105
  265.3 3.0 fusion.105
  272.0 3.0 fusion.105
  278.7 3.0 fusion.105
  285.4 3.0 fusion.105
  292.1 3.0 fusion.105
  298.8 3.0 fusion.105
  305.5 3.0 fusion.105
  312.1 3.0 fusion.105
  318.8 3.0 fusion.105
  325.5 3.0 fusion.105
  332.3 170.2 %all-reduce.2.cloned.1.call-done = f32[512,1024]{1,0:T(8,128)} async-done(((f32[512,1024]{1,0:T(8,128)}), f32[512,1024]{1,0:T(8,128)}) %all-reduce.2.cloned.1.call-update) | async-done | bytes 2097168 | tf_op jit(solution)/shard_map/psum | solution.py:174
  504.0 89.6 %all-gather.9.cloned.1.call-done = bf16[6144,512]{1,0:T(8,128)(2,1)} async-done(((bf16[192,512]{1,0:T(8,128)(2,1)}), bf16[6144,512]{1,0:T(8,128)(2,1)}) %all-gather.9.cloned.1.call-update) | async-done | bytes 6291472 | tf_op jit(solution)/shard_map/all_gather | solution.py:135
  593.6 88.1 %all-gather.11.cloned.1.call-done = bf16[6144,512]{1,0:T(8,128)(2,1)} async-done(((bf16[192,512]{1,0:T(8,128)(2,1)}), bf16[6144,512]{1,0:T(8,128)(2,1)}) %all-gather.11.cloned.1.call-update) | async-done | bytes 6291472 | tf_op jit(solution)/shard_map/all_gather | solution.py:136
  681.7 135.7 %while.46 = (s32[]{:T(128)}, f32[192,4,128]{2,0,1:T(8,128)}, f32[192,4,128]{2,0,1:T(8,128)}, bf16[6144,512]{1,0:T(8,128)(2,1)}, bf16[6144,512]{1,0:T(8,128)(2,1)...) while((s32[]{:T(128)}, f32[192,4,128]{2,0,1:T(8,128)}, ...), condition=%wide.region_16.17_spmd.clone, body=%wide.region_13.16_spmd.clone.sunk | while | flops 410231040 | bytes 20461572 | solution.py:165
  683.2 2.5 convolution_multiply_fusion.2
  687.0 3.5 fusion.112
  694.4 2.5 convolution_multiply_fusion.2
  698.2 3.6 fusion.112
  705.7 2.5 convolution_multiply_fusion.2
  709.5 3.6 fusion.112
  717.0 2.5 convolution_multiply_fusion.2
  720.8 3.6 fusion.112
  728.3 2.5 convolution_multiply_fusion.2
  732.2 3.6 fusion.112
  739.7 2.5 convolution_multiply_fusion.2
  743.5 3.6 fusion.112
  751.0 2.5 convolution_multiply_fusion.2
  754.8 3.6 fusion.112
  762.3 2.5 convolution_multiply_fusion.2
  766.1 3.6 fusion.112
  769.7 2.5 fusion.113
  773.7 2.5 convolution_multiply_fusion.2
  777.5 3.6 fusion.112
  785.0 2.5 convolution_multiply_fusion.2
  788.8 3.6 fusion.112
  796.3 2.5 convolution_multiply_fusion.2
  800.1 3.6 fusion.112
  807.6 2.5 convolution_multiply_fusion.2
  811.4 3.6 fusion.112
  815.0 2.5 fusion.113
  (346 shorter events, 162.5 us)
Async XLA Ops:
  7.2 234.6 %copy-start = (bf16[512,1024]{1,0:T(8,128)(2,1)S(1)}, bf16[512,1024]{1,0:T(8,128)(2,1)}, u32[]{:S(2)}) copy-start(bf16[512,1024]{1,0:T(8,128)(2,1)} %param.19) | copy-start | bytes 3145732
  7.2 95.6 %all-gather.5.cloned.1.call-start = ((), (), s32[]{:S(2)}) async-start(), calls=%async_computation | async-start | bytes 6488064 | tf_op jit(solution)/shard_map/all_gather | solution.py:70
  7.9 183.2 %all-gather.7.cloned.1.call-start = ((), (), s32[]{:S(2)}) async-start(), calls=%async_computation.1 | async-start | bytes 6488064 | tf_op jit(solution)/shard_map/all_gather | solution.py:69
  8.7 493.9 %all-reduce.2.cloned.1.call-start = ((), (), s32[]{:S(2)}) async-start(), calls=%async_computation.4 | async-start | bytes 4194304 | tf_op jit(solution)/shard_map/psum | solution.py:174
  199.7 42.1 %copy-start.4 = (bf16[192,1024]{1,0:T(8,128)(2,1)S(1)}, bf16[192,1024]{1,0:T(8,128)(2,1)}, u32[]{:S(2)}) copy-start(bf16[192,1024]{1,0:T(8,128)(2,1)} %param.20) | copy-start | bytes 1179652
  199.7 42.1 %copy-start.7 = (bf16[192,512]{1,0:T(8,128)(2,1)S(1)}, bf16[192,512]{1,0:T(8,128)(2,1)}, u32[]{:S(2)}) copy-start(bf16[192,512]{1,0:T(8,128)(2,1)} %param.17) | copy-start | bytes 589828
  199.7 42.1 %copy-start.8 = (f32[512]{0:T(512)S(1)}, f32[512]{0:T(512)}, u32[]{:S(2)}) copy-start(f32[512]{0:T(512)} %param.18) | copy-start | bytes 6148
  243.4 1.8 copy-start.3
  243.4 4.1 copy-start.2
  245.2 0.9 copy-start.5
  245.2 1.6 copy-start.6
  245.2 348.4 %all-gather.9.cloned.1.call-start = ((), (), s32[]{:S(2)}) async-start(), calls=%async_computation.2 | async-start | bytes 6488064 | tf_op jit(solution)/shard_map/all_gather | solution.py:135
  245.8 435.9 %all-gather.11.cloned.1.call-start = ((), (), s32[]{:S(2)}) async-start(), calls=%async_computation.3 | async-start | bytes 6488064 | tf_op jit(solution)/shard_map/all_gather | solution.py:136
  687.0 3.5 copy-start.1
  698.2 3.6 copy-start.1
  709.5 3.6 copy-start.1
  720.8 3.6 copy-start.1
  732.2 3.6 copy-start.1
  743.5 3.6 copy-start.1
  754.8 3.6 copy-start.1
  766.1 3.6 copy-start.1
  777.5 3.6 copy-start.1
  788.8 3.6 copy-start.1
  800.1 3.6 copy-start.1
  811.4 3.6 copy-start.1
Sparse Core Ops, SparseCore 0:
  10.6 92.1 all-gather.4
  105.4 85.6 all-gather.6
  245.3 257.1 all-reduce.1
  505.0 88.5 all-gather.8
  596.0 85.6 all-gather.10
where the time goes:
time: 830 us; the launch traced here: 827 us
  waiting for transfers between devices  521 us (63%)
  matrix products  179 us (22%)
  local copies, waits for them, and re-layouts  91.9 us (11%)
  other arithmetic  19.6 us (2%)
  between operations  13.9 us (2%)
    psum x1, waiting for transfers between devices, per_device(): summed = lax.psum(full_term, ('dp', 'seq'))  170 us
    all_gather x1, waiting for transfers between devices, per_device(): lax.all_gather(value_vectors, 'seq', axis=0, tiled=True)  91.6 us
    all_gather x1, waiting for transfers between devices, per_device(): query_piece = lax.all_gather(queries, 'seq', axis=0, tiled=True)  89.6 us
    all_gather x1, waiting for transfers between devices, per_device(): grad_piece = lax.all_gather(attn_grad, 'seq', axis=0, tiled=True)  88.1 us
    all_gather x1, waiting for transfers between devices, per_device(): lax.all_gather(key_vectors, 'seq', axis=0, tiled=True)  79.6 us
    dot_general x24, matrix products, score_block(): jnp.einsum('qhd,khd->hqk', query_heads, key_heads, preferred_element_type...  45 us
    dot_general x12, matrix products, inner(): jnp.einsum('hqk,qhd->khd', grad_scores, piece_heads, preferred_element_ty...  42.6 us
    dot_general x12, matrix products, backward_step(): jnp.einsum('hqk,khd->qhd', grad_scores, key_heads, preferred_element_type...  35.8 us
  transfers between devices with their start and end apart: 5, of which 5 were waited for; matrix products, arithmetic and copies ran while one was open for 12% of the time, Pallas kernels for 0%

commit v1 on v0

v1 whole, which is shorter than its diff:
```python
import jax
import jax.numpy as jnp
from jax import lax
from jax.experimental import pallas as pl
from jax.experimental.pallas import tpu as pltpu
from jax.sharding import PartitionSpec as P

TOK = 192
HEAD = 128
HEADS = 4
QK = HEAD * HEADS
WIDTH = 1024
SLOTS = 4
YN = 4
ZN = 8
CHUNK = YN * TOK
SCALE = HEAD ** (-0.5)
EPS = 1e-5
ALL_ROWS = 49152
BF = jnp.bfloat16
F32 = jnp.float32
MESH = pl.DeviceIdType.MESH
NT = (((1,), (1,)), ((), ()))
NN = (((1,), (0,)), ((), ()))


def dot(a, b, dims=NN):
    return lax.dot_general(a, b, dims, preferred_element_type=F32)


def layer_kernel(
    q_ref, k_ref, v_ref, u_ref, og_ref, w_ref, gain_ref, gain_heads_ref, ends_ref,
    lay_ref, dq_ref, dk_ref, dv_ref, gg_out_ref, wg_ref,
    k_all, v_all, q_blk, gh_blk, gh_own, gg, ends_sib, att, stat,
    nrm_blk, do_blk, nrm_in, dq_acc, dq_blk,
    part_out, part_in, part_own, red, ring_in, ring_acc, fin,
    w_part, w_sib, w_sum, w_x, w_64, w_y, w_16, w_z,
    a_send, a_recv, y_send, y_recv, s_send, s_recv, e_sem, t_send, t_recv, n_send, n_recv,
    p_send, p_recv, r_send, r_recv, f_send, f_recv,
    ws_sem, wx_send, wx_recv, wy_send, wy_recv, wz_send, wz_recv, wb_send, wb_recv,
):
    d = lax.axis_index("dp")
    s = lax.axis_index("seq")
    x, c = d // 2, d % 2
    z, y = s // YN, s % YN
    row, head = z // HEADS, z % HEADS
    core_of_z = ((z + 1) // 2) % 2
    slot_of_z = z // 2
    right, left, across = (y + 1) % YN, (y + 3) % YN, (y + 2) % YN

    def zmap(core, j):
        return 2 * j + core if j % 2 == 0 else 2 * j + 1 - core

    def at(core, zz, yy):
        return (2 * x + core, YN * zz + yy)

    sibling = at(1 - c, z, y)
    to_right, to_left = at(c, z, right), at(c, z, left)

    def remote(src, dst, send, recv, device):
        return pltpu.make_async_remote_copy(
            src_ref=src, dst_ref=dst, send_sem=send, recv_sem=recv,
            device_id=device, device_id_type=MESH,
        )

    def landed(dst, sem):
        pltpu.make_async_copy(dst, dst, sem).wait()

    home = [(at(core_of_z, HEADS * c + h, y), (core_of_z == c) & (HEADS * c + h == z)) for h in range(HEADS)]
    owner = [(at(row, zmap(c, j), y), (row == c) & (zmap(c, j) == z)) for j in range(SLOTS)]
    own_z = [zmap(c, j) for j in range(SLOTS)]
    sib_z = [zmap(1 - c, j) for j in range(SLOTS)]

    bar = pltpu.get_barrier_semaphore()

    def greet(device):
        pl.semaphore_signal(bar, inc=1, device_id=device, device_id_type=MESH)

    for device, mine in home + owner:
        @pl.when(jnp.logical_not(mine))
        def _():
            greet(device)
    for step in range(1, YN):
        greet(at(c, z, (y + step) % YN))
        greet((2 * ((x + step) % 4) + c, s))
    greet(sibling)
    for h in range(HEADS):
        @pl.when(h != head)
        def _():
            greet(at(c, HEADS * row + h, y))
    collector = z == d

    @pl.when(collector)
    def _():
        for zz in range(ZN):
            @pl.when(zz != z)
            def _():
                greet((d, YN * zz + y))

    @pl.when(jnp.logical_not(collector))
    def _():
        greet((z, s))

    selfs = (home[0][1] | home[1][1] | home[2][1] | home[3][1]).astype(jnp.int32)
    pl.semaphore_wait(bar, 8 - 2 * selfs + 3 + 3 + 1 + 3 + jnp.where(collector, ZN - 1, 1))

    block = YN * z + y

    def scatter(a, src, dst):
        for h in range(HEADS):
            device, mine = home[h]
            cols = src.at[:, h * HEAD:(h + 1) * HEAD]

            @pl.when(mine)
            def _():
                pltpu.make_async_copy(cols, dst, a_recv.at[a, slot_of_z]).start()

            @pl.when(jnp.logical_not(mine))
            def _():
                remote(cols, dst, a_send.at[a, h], a_recv.at[a, slot_of_z], device).start()

    remote(ends_ref, ends_sib, e_sem.at[0], e_sem.at[1], sibling).start()
    scatter(0, k_ref, k_all.at[block])
    scatter(1, v_ref, v_all.at[block])
    scatter(2, q_ref, q_blk.at[slot_of_z])
    gg[...] = dot(og_ref[...], w_ref[...], NT)
    gh_own[...] = (gg[...] * u_ref[...].astype(F32) * gain_ref[...]).astype(BF)
    scatter(3, gh_own, gh_blk.at[slot_of_z])

    kv = (k_all, v_all)
    for j in range(SLOTS):
        for a in range(2):
            ref = kv[a].at[YN * own_z[j] + y]
            landed(ref, a_recv.at[a, j])
            remote(ref, ref, y_send.at[a, j, 0], y_recv.at[a, j, 0], to_right).start()
            remote(ref, ref, y_send.at[a, j, 1], y_recv.at[a, j, 1], to_left).start()
    for j in range(SLOTS):
        ref = k_all.at[YN * own_z[j] + left]
        landed(ref, y_recv.at[0, j, 0])
        remote(ref, ref, y_send.at[0, j, 2], y_recv.at[0, j, 2], to_right).start()
        ref = v_all.at[YN * own_z[j] + right]
        landed(ref, y_recv.at[1, j, 1])
        remote(ref, ref, y_send.at[1, j, 2], y_recv.at[1, j, 2], to_left).start()

    landed(ends_sib, e_sem.at[1])
    ends = jnp.where(row == c, ends_ref[...], ends_sib[...])

    def start_of(place, e0, e1, e2):
        return jnp.where(place >= e2, e2, jnp.where(place >= e1, e1, jnp.where(place >= e0, e0, 0)))

    for j in range(SLOTS):
        landed(q_blk.at[j], a_recv.at[2, j])
    att[...] = jnp.zeros_like(att)

    def attend(j, zq, zk):
        place = (YN * zq + y) * TOK + lax.broadcasted_iota(jnp.int32, (TOK, 1), 0)
        begin = start_of(place, ends[0:1, 0:1], ends[1:2, 0:1], ends[2:3, 0:1])
        keys = k_all[pl.ds(YN * zk, YN)].reshape(CHUNK, HEAD)
        values = v_all[pl.ds(YN * zk, YN)].reshape(CHUNK, HEAD)
        half = dot(q_blk[j], keys, NT) * (0.5 * SCALE)
        key_place = zk * CHUNK + lax.broadcasted_iota(jnp.int32, (TOK, CHUNK), 1)
        visible = (key_place <= place) & (key_place >= begin)
        weights = jnp.where(visible, half * (1.0 + jnp.tanh(half)), 0.0).astype(BF)
        att[j] += dot(weights, values)

    def zmap_at(core, j):
        return 2 * j + jnp.where(j % 2 == 0, core, 1 - core)

    def forward(zk, first):
        def step(j, carry):
            attend(j, zmap_at(c, j), zk)
            return carry
        lax.fori_loop(first, SLOTS, step, 0)

    for j in range(SLOTS):
        for a in range(2):
            for n, yy in ((0, left), (1, right), (2, across)):
                if (a, n) in ((0, 0), (1, 1)):
                    continue
                landed(kv[a].at[YN * own_z[j] + yy], y_recv.at[a, j, n])
            ref = kv[a].at[pl.ds(YN * own_z[j], YN)]
            remote(ref, ref, s_send.at[a, j], s_recv.at[a, j], sibling).start()
        forward(own_z[j], j)
    for j in range(SLOTS):
        for a in range(2):
            landed(kv[a].at[pl.ds(YN * sib_z[j], YN)], s_recv.at[a, j])
        forward(sib_z[j], j + (own_z[j] < sib_z[j]).astype(jnp.int32))

    for j in range(SLOTS):
        landed(gh_blk.at[j], a_recv.at[3, j])
    flat_att = att[...].reshape(SLOTS * TOK, HEAD)
    flat_gh = gh_blk[...].reshape(SLOTS * TOK, HEAD).astype(F32)
    head_mean = jnp.mean(flat_att, axis=1, keepdims=True)
    centred = flat_att - head_mean
    lane = lax.broadcasted_iota(jnp.int32, (SLOTS * TOK, HEAD), 1)
    packed = jnp.where(lane == 0, head_mean, 0.0)
    packed = jnp.where(lane == 1, jnp.sum(centred * centred, axis=1, keepdims=True), packed)
    packed = jnp.where(lane == 2, jnp.sum(flat_gh * centred, axis=1, keepdims=True), packed)
    packed = jnp.where(lane == 3, jnp.sum(flat_gh, axis=1, keepdims=True), packed)
    stat[head] = jnp.transpose(packed)[0:8]
    for h in range(HEADS):
        @pl.when(h != head)
        def _():
            remote(stat.at[head], stat.at[head], t_send.at[h], t_recv.at[head],
                   at(c, HEADS * row + h, y)).start()
    for h in range(HEADS):
        @pl.when(h != head)
        def _():
            landed(stat.at[h], t_recv.at[h])
    means = [stat[h, 0:1, :] for h in range(HEADS)]
    grads = [stat[h, 3:4, :] for h in range(HEADS)]
    mean = (means[0] + means[1] + means[2] + means[3]) * (1.0 / HEADS)
    square, cross, grad_sum = 0.0, 0.0, 0.0
    for h in range(HEADS):
        off = means[h] - mean
        square += stat[h, 1:2, :] + HEAD * off * off
        cross += stat[h, 2:3, :] + off * grads[h]
        grad_sum += grads[h]
    inv_std = 1.0 / jnp.sqrt(square * (1.0 / QK) + EPS)
    rows = jnp.concatenate(
        [mean, inv_std, grad_sum * (1.0 / QK), cross * inv_std * (1.0 / QK),
         jnp.zeros((HEAD - 4, SLOTS * TOK), F32)], axis=0)
    cols = jnp.transpose(rows)
    mean_c, inv_c, gmean_c, proj_c = (cols[:, i:i + 1] for i in range(4))
    unit = (flat_att - mean_c) * inv_c
    nrm_blk[...] = (unit * gain_heads_ref[head]).astype(BF).reshape(SLOTS, TOK, HEAD)
    do_blk[...] = (inv_c * (flat_gh - gmean_c - unit * proj_c)).astype(BF).reshape(SLOTS, TOK, HEAD)

    head_cols = pl.ds(pl.multiple_of(head * HEAD, HEAD), HEAD)

    def give_back(src, dst, send, recv, j):
        device, mine = owner[j]

        @pl.when(mine)
        def _():
            pltpu.make_async_copy(src, dst, recv).start()

        @pl.when(jnp.logical_not(mine))
        def _():
            remote(src, dst, send, recv, device).start()

    for j in range(SLOTS):
        give_back(nrm_blk.at[j], nrm_in.at[:, head_cols], n_send.at[j], n_recv.at[head], j)

    lanes = lax.broadcasted_iota(jnp.int32, (1, SLOTS * TOK), 1)
    slot_z = jnp.where(lanes < TOK, own_z[0], jnp.where(
        lanes < 2 * TOK, own_z[1], jnp.where(lanes < 3 * TOK, own_z[2], own_z[3])))
    slot_n = jnp.where(lanes < TOK, 0, jnp.where(lanes < 2 * TOK, 1, jnp.where(lanes < 3 * TOK, 2, 3)))
    query_place = (YN * slot_z + y) * TOK + lanes - slot_n * TOK
    query_begin = start_of(query_place, ends[0:1], ends[1:2], ends[2:3])
    dq_acc[...] = jnp.zeros_like(dq_acc)

    def backward(zk, first, store):
        width = (SLOTS - first) * TOK
        lo = first * TOK
        queries = q_blk[first:].reshape(width, HEAD)
        grads_out = do_blk[first:].reshape(width, HEAD)
        place, begin = query_place[:, lo:], query_begin[:, lo:]

        def step(b, carry):
            keys = k_all[YN * zk + b]
            values = v_all[YN * zk + b]
            half = dot(keys, queries, NT) * (0.5 * SCALE)
            gw = dot(values, grads_out, NT)
            t = jnp.tanh(half)
            plus = 1.0 + t
            key_place = (YN * zk + b) * TOK + lax.broadcasted_iota(jnp.int32, (TOK, width), 0)
            visible = (key_place <= place) & (key_place >= begin)
            weights = jnp.where(visible, half * plus, 0.0).astype(BF)
            ds = jnp.where(visible, gw * plus * (1.0 + half * (1.0 - t)), 0.0).astype(BF)
            store(b, dot(ds, queries), dot(weights, grads_out))
            dq_acc[:, lo:] += dot(jnp.transpose(keys), ds)
            return carry

        lax.fori_loop(0, YN, step, 0)

    def backward_sib(j):
        def store(b, dk, dv):
            part_out[0, j, b] = dk.astype(BF)
            part_out[1, j, b] = dv.astype(BF)

        full = own_z[j] > sib_z[j]

        @pl.when(full)
        def _():
            backward(sib_z[j], j, store)

        @pl.when(jnp.logical_not(full))
        def _():
            if j + 1 < SLOTS:
                backward(sib_z[j], j + 1, store)
            else:
                for a in range(2):
                    part_out[a, j] = jnp.zeros((YN, TOK, HEAD), BF)

        for a in range(2):
            remote(part_out.at[a, j], part_in.at[a, j], p_send.at[a, j], p_recv.at[a, j], sibling).start()

    def backward_own(j):
        def store(b, dk, dv):
            part_own[0, b] = dk
            part_own[1, b] = dv

        backward(own_z[j], j, store)

    def chip_sum(j):
        for a in range(2):
            landed(part_in.at[a, j], p_recv.at[a, j])
            red[a, j] = (part_own[a] + part_in[a, j].astype(F32)).astype(BF)
        ring(0, j, red.at[0, j, across], to_right)
        ring(1, j, red.at[1, j, across], to_left)
        ring(2, j, red.at[1, j, right], to_right)
        ring(3, j, red.at[0, j, left], to_left)

    def ring(n, j, src, device):
        remote(src, ring_in.at[n, j], r_send.at[n, j], r_recv.at[n, j], device).start()

    def relay(j):
        landed(ring_in.at[0, j], r_recv.at[0, j])
        ring_acc[0, j] = (red[0, j, right].astype(F32) + ring_in[0, j].astype(F32)).astype(BF)
        ring(4, j, ring_acc.at[0, j], to_right)
        landed(ring_in.at[1, j], r_recv.at[1, j])
        ring_acc[1, j] = (red[1, j, left].astype(F32) + ring_in[1, j].astype(F32)).astype(BF)
        ring(5, j, ring_acc.at[1, j], to_left)

    def finish(j):
        for n in (2, 3, 4, 5):
            landed(ring_in.at[n, j], r_recv.at[n, j])
        fin[0, j] = ((red[0, j, y].astype(F32) + ring_in[3, j].astype(F32) + ring_in[4, j].astype(F32))
                     * (0.5 * SCALE)).astype(BF)
        fin[1, j] = (red[1, j, y].astype(F32) + ring_in[2, j].astype(F32)
                     + ring_in[5, j].astype(F32)).astype(BF)
        give_back(fin.at[0, j], dk_ref.at[:, head_cols], f_send.at[0, j], f_recv.at[0, head], j)
        give_back(fin.at[1, j], dv_ref.at[:, head_cols], f_send.at[1, j], f_recv.at[1, head], j)

    def project():
        for h in range(HEADS):
            landed(nrm_in.at[:, h * HEAD:(h + 1) * HEAD], n_recv.at[h])
        normed = nrm_in[...].astype(F32)
        gated = (normed * u_ref[...].astype(F32)).astype(BF)
        gg_out_ref[...] = (gg[...] * normed).astype(BF)
        w_part[...] = dot(jnp.transpose(gated), og_ref[...]).astype(BF).reshape(4, 2, 64, WIDTH)
        remote(w_part.at[:, 1 - c], w_sib, ws_sem.at[0], ws_sem.at[1], sibling).start()
        lay_ref[...] = dot(gated, w_ref[...]).astype(BF)

    def weight_x():
        landed(w_sib, ws_sem.at[1])
        w_sum[...] = (w_part[:, c].astype(F32) + w_sib[...].astype(F32)).astype(BF)
        for step in range(1, 4):
            to = (x + step) % 4
            remote(w_sum.at[to], w_x.at[step - 1], wx_send.at[step - 1], wx_recv.at[step - 1],
                   (2 * to + c, s)).start()

    def weight_y():
        total = w_sum[x].astype(F32)
        for step in range(3):
            landed(w_x.at[step], wx_recv.at[step])
            total += w_x[step].astype(F32)
        w_64[...] = total.astype(BF).reshape(YN, 16, WIDTH)
        for step in range(1, YN):
            to = (y + step) % YN
            remote(w_64.at[to], w_y.at[step - 1], wy_send.at[step - 1], wy_recv.at[step - 1],
                   at(c, z, to)).start()

    def weight_z():
        total = w_64[y].astype(F32)
        for step in range(3):
            landed(w_y.at[step], wy_recv.at[step])
            total += w_y[step].astype(F32)
        w_16[...] = total.astype(BF)

        @pl.when(jnp.logical_not(collector))
        def _():
            remote(w_16, w_z.at[z], wz_send, wz_recv.at[z], (d, YN * d + y)).start()

    def weight_all():
        @pl.when(collector)
        def _():
            w_z[z] = w_16[...]
            for zz in range(ZN):
                @pl.when(zz != z)
                def _():
                    landed(w_z.at[zz], wz_recv.at[zz])
            total = w_z[0].astype(F32)
            for zz in range(1, ZN):
                total += w_z[zz].astype(F32)
            wg_ref[...] = total * (ALL_ROWS ** (-0.5))
            for dd in range(8):
                @pl.when(dd != d)
                def _():
                    remote(wg_ref, wg_ref, wb_send.at[dd], wb_recv, (dd, s)).start()

    backward_sib(3)
    backward_own(3)
    chip_sum(3)
    project()
    backward_sib(2)
    relay(3)
    backward_own(2)
    chip_sum(2)
    weight_x()
    finish(3)
    backward_sib(1)
    relay(2)
    weight_y()
    backward_own(1)
    chip_sum(1)
    finish(2)
    weight_z()
    backward_sib(0)
    relay(1)
    backward_own(0)
    chip_sum(0)
    finish(1)
    dq_blk[...] = (jnp.transpose(dq_acc[...]) * (0.5 * SCALE)).astype(BF).reshape(SLOTS, TOK, HEAD)
    for j in range(SLOTS):
        give_back(dq_blk.at[j], dq_ref.at[:, head_cols], f_send.at[2, j], f_recv.at[2, head], j)
    weight_all()
    relay(0)
    finish(0)

    for a, dst in ((0, dk_ref), (1, dv_ref), (2, dq_ref)):
        for h in range(HEADS):
            landed(dst.at[:, h * HEAD:(h + 1) * HEAD], f_recv.at[a, h])

    @pl.when(collector)
    def _():
        for dd in range(8):
            @pl.when(dd != d)
            def _():
                remote(wg_ref, wg_ref, wb_send.at[dd], wb_recv, (dd, s)).wait_send()

    @pl.when(jnp.logical_not(collector))
    def _():
        landed(wg_ref, wb_recv)
        remote(w_16, w_z.at[z], wz_send, wz_recv.at[z], (d, YN * d + y)).wait_send()

    def sent(src, sem):
        pltpu.make_async_copy(src, src, sem).wait()

    sent(ends_ref, e_sem.at[0])
    sent(w_part.at[:, 1 - c], ws_sem.at[0])
    for h in range(HEADS):
        @pl.when(jnp.logical_not(home[h][1]))
        def _():
            for a in range(4):
                sent(q_blk.at[0], a_send.at[a, h])

        @pl.when(h != head)
        def _():
            sent(stat.at[head], t_send.at[h])
    for j in range(SLOTS):
        @pl.when(jnp.logical_not(owner[j][1]))
        def _():
            sent(nrm_blk.at[j], n_send.at[j])
            for a in range(3):
                sent(dq_blk.at[j], f_send.at[a, j])
        for a in range(2):
            for n in range(3):
                sent(q_blk.at[0], y_send.at[a, j, n])
            sent(part_out.at[a, j], s_send.at[a, j])
            sent(part_out.at[a, j], p_send.at[a, j])
        for n in range(6):
            sent(ring_in.at[n, j], r_send.at[n, j])
    for step in range(3):
        sent(w_x.at[step], wx_send.at[step])
        sent(w_y.at[step], wy_send.at[step])


def per_device(queries, keys, values, gates, gain, out_weight, out_grad, lengths):
    ends = jnp.cumsum(lengths[0])[:, None]
    ends = jnp.broadcast_to(jnp.concatenate([ends, ends], axis=0), (8, SLOTS * TOK)).astype(jnp.int32)
    vm = pl.BlockSpec(memory_space=pltpu.VMEM)
    block = (SLOTS, TOK, HEAD)
    dma = pltpu.SemaphoreType.DMA
    scratch = [
        pltpu.VMEM((ZN * YN, TOK, HEAD), BF),
        pltpu.VMEM((ZN * YN, TOK, HEAD), BF),
        pltpu.VMEM(block, BF),
        pltpu.VMEM(block, BF),
        pltpu.VMEM((TOK, QK), BF),
        pltpu.VMEM((TOK, QK), F32),
        pltpu.VMEM((8, SLOTS * TOK), jnp.int32),
        pltpu.VMEM(block, F32),
        pltpu.VMEM((HEADS, 8, SLOTS * TOK), F32),
        pltpu.VMEM(block, BF),
        pltpu.VMEM(block, BF),
        pltpu.VMEM((TOK, QK), BF),
        pltpu.VMEM((HEAD, SLOTS * TOK), F32),
        pltpu.VMEM(block, BF),
        pltpu.VMEM((2, SLOTS, YN, TOK, HEAD), BF),
        pltpu.VMEM((2, SLOTS, YN, TOK, HEAD), BF),
        pltpu.VMEM((2, YN, TOK, HEAD), F32),
        pltpu.VMEM((2, SLOTS, YN, TOK, HEAD), BF),
        pltpu.VMEM((6, SLOTS, TOK, HEAD), BF),
        pltpu.VMEM((2, SLOTS, TOK, HEAD), BF),
        pltpu.VMEM((2, SLOTS, TOK, HEAD), BF),
        pltpu.VMEM((4, 2, 64, WIDTH), BF),
        pltpu.VMEM((4, 64, WIDTH), BF),
        pltpu.VMEM((4, 64, WIDTH), BF),
        pltpu.VMEM((3, 64, WIDTH), BF),
        pltpu.VMEM((YN, 16, WIDTH), BF),
        pltpu.VMEM((3, 16, WIDTH), BF),
        pltpu.VMEM((16, WIDTH), BF),
        pltpu.VMEM((ZN, 16, WIDTH), BF),
        dma((4, 4)), dma((4, 4)),
        dma((2, 4, 3)), dma((2, 4, 3)),
        dma((2, 4)), dma((2, 4)),
        dma((2,)),
        dma((4,)), dma((4,)),
        dma((4,)), dma((4,)),
        dma((2, 4)), dma((2, 4)),
        dma((6, 4)), dma((6, 4)),
        dma((3, 4)), dma((3, 4)),
        dma((2,)),
        dma((3,)), dma((3,)),
        dma((3,)), dma((3,)),
        dma, dma((8,)),
        dma((8,)), dma,
    ]
    return pl.pallas_call(
        layer_kernel,
        out_shape=(
            jax.ShapeDtypeStruct((TOK, WIDTH), BF),
            jax.ShapeDtypeStruct((TOK, QK), BF),
            jax.ShapeDtypeStruct((TOK, QK), BF),
            jax.ShapeDtypeStruct((TOK, QK), BF),
            jax.ShapeDtypeStruct((TOK, QK), BF),
            jax.ShapeDtypeStruct((16, WIDTH), F32),
        ),
        in_specs=[vm] * 9,
        out_specs=(vm,) * 6,
        scratch_shapes=scratch,
        compiler_params=pltpu.CompilerParams(
            collective_id=0, has_side_effects=True, vmem_limit_bytes=56 * 1024 * 1024
        ),
    )(
        queries, keys, values, gates, out_grad, out_weight,
        gain.reshape(1, QK), gain.reshape(HEADS, 1, HEAD), ends,
    )


def solution(mesh):
    rows = P(("dp", "seq"), None)

    def program(queries, keys, values, gates, gain, out_weight, out_grad, lengths):
        return jax.shard_map(
            per_device,
            mesh=mesh,
            in_specs=(rows, rows, rows, rows, P(), P(), rows, P("dp", None)),
            out_specs=(rows, rows, rows, rows, rows, P("seq", None)),
            check_vma=False,
        )(queries, keys, values, gates, gain, out_weight, out_grad, lengths)

    return program
```

time: 830 us -> 105 us (0.13)
  waiting for transfers between devices: 521 us -> 0 us
  matrix products: 179 us -> 0 us
  Pallas kernels: 0 us -> 96.4 us
  local copies, waits for them, and re-layouts: 91.9 us -> 7.62 us
  other arithmetic: 19.6 us -> 0.25 us
  between operations: 13.9 us -> 0.67 us
    all_gather x4 -> x0, waiting for transfers between devices: 349 us -> none  [the longest x1 91.6 us: per_device(): lax.all_gather(value_vectors, 'seq', axis=0, tiled=True)]
    dot_general x75 -> x0, matrix products: 179 us -> none  [the longest x24 45 us: score_block(): jnp.einsum('qhd,khd->hqk', query_heads, key_heads, preferred_element_type...]
    psum x1 -> x0, waiting for transfers between devices: 170 us -> none  [per_device(): summed = lax.psum(full_term, ('dp', 'seq'))]
    pallas_call x0 -> x1, Pallas kernels: none -> 96.4 us  [per_device(): pl.pallas_call(layer_kernel, out_shape=(jax.ShapeDtypeStruct((TOK, WIDTH)...]
    dynamic_slice x60 -> x0, local copies, waits for them, and re-layouts: 70.4 us -> none  [the longest x24 27.3 us: inner(): lax.dynamic_slice_in_dim(grad_piece, offset, sub_rows, 0)]
    unnamed x22 -> x18, local copies, waits for them, and re-layouts: 21.4 us -> 6.94 us
    convert_element_type x40 -> x0, other arithmetic: 10.4 us -> none  [the longest x36 4.39 us: score_block(): (same_owner & (query_places[:, None] >= key_places[None, :])).astype(jnp....]
  transfers between devices with their start and end apart: 5 -> 0, of which waited for: 5 -> 0; matrix products, arithmetic and copies ran while one was open for 12% -> 0% of each run, Pallas kernels for 0% -> 0%
where the time goes in v1:
time: 105 us
  Pallas kernels  96.4 us (92%)
  local copies, waits for them, and re-layouts  7.62 us (7%)
    pallas_call x1, Pallas kernels, per_device(): pl.pallas_call(layer_kernel, out_shape=(jax.ShapeDtypeStruct((TOK, WIDTH)...  96.4 us
    unnamed x18, local copies, waits for them, and re-layouts  6.94 us

profile of v1, /device:TPU:1, one launch (start us, length us, event | category | flops | bytes accessed | tf_op | source)
XLA Modules:
  0.0 104.9 jit_solution(12419710447299859203)
XLA Ops:
  0.6 0.0 copy-start.5
  0.6 0.6 copy-done.5
  1.3 0.2 reduce-window_clone.1
  1.5 0.1 add_bitcast_fusion
  1.5 0.7 broadcast_in_dim.9.ends_ref
  2.2 96.4 %shard_map.127 = (bf16[192,1024]{1,0:T(8,128)(2,1)}, bf16[192,512]{1,0:T(8,128)(2,1)}, bf16[192,512]{1,0:T(8,128)(2,1)}, bf16[192,512]{1,0:T(8,128)(2,1)}, bf16[192,512]{1,0:T(8,128)(2,1)}, /*index=5*/f32[16,1024]{1,0:T(8,128)}) custom-call(bf16[192,512]{1,0:T(8,128)(2,1)} %q_ref.1, bf16[192,512]{1,0:T(8,128)(2,1)} %k_ref.1, bf16[192,512]{1,0:T(8,128)(2,1)} %v_ref.1, ...), custom_call_target="tpu_custom_call" | custom-call | tf_op jit(solution)/shard_map/pallas_call | solution.py:521
  98.6 0.0 copy-start.3
  98.6 1.8 %copy.20 = bf16[192,1024]{1,0:T(8,128)(2,1)} copy(bf16[192,1024]{1,0:T(8,128)(2,1)} %get-tuple-element.12) | data formatting | bytes 786432
  100.4 0.0 copy-done.3
  100.4 0.0 copy-start.2
  100.4 0.7 copy.21
  101.1 0.3 copy-done.2
  101.4 0.0 copy-start.1
  101.4 0.7 copy.22
  102.1 0.3 copy-done.1
  102.4 0.0 copy-start
  102.4 0.7 copy.23
  103.1 0.3 copy-done
  103.4 0.0 copy-start.4
  103.4 0.7 copy.24
  104.1 0.2 copy-done.4
  104.3 0.6 copy.25
Async XLA Ops:
  0.6 0.7 copy-start.5
  98.6 1.8 %copy-start.3 = (bf16[192,512]{1,0:T(8,128)(2,1)S(1)}, bf16[192,512]{1,0:T(8,128)(2,1)}, u32[]{:S(2)}) copy-start(bf16[192,512]{1,0:T(8,128)(2,1)} %get-tuple-element.13) | copy-start | bytes 589828
  100.4 1.0 copy-start.2
  101.4 1.0 copy-start.1
  102.4 1.0 copy-start
  103.4 0.9 copy-start.4

commit v2 on v1

v2 whole, which is shorter than its diff:
```python
import jax
import jax.numpy as jnp
from jax import lax
from jax.experimental import pallas as pl
from jax.experimental.pallas import tpu as pltpu
from jax.sharding import PartitionSpec as P

TOK = 192
HEAD = 128
HEADS = 4
QK = HEAD * HEADS
WIDTH = 1024
SLOTS = 4
YN = 4
ZN = 8
CHUNK = SLOTS * TOK
PAIR = 2 * TOK
SCALE = HEAD ** (-0.5)
EPS = 1e-5
ALL_ROWS = 49152
BF = jnp.bfloat16
F32 = jnp.float32
MESH = pl.DeviceIdType.MESH
NT = (((1,), (1,)), ((), ()))
NN = (((1,), (0,)), ((), ()))


def dot(a, b, dims=NN):
    return lax.dot_general(a, b, dims, preferred_element_type=F32)


def layer_kernel(
    q_ref, k_ref, v_ref, u_hbm, og_hbm, w_hbm, gain_ref, len_ref,
    lay_ref, dq_ref, dk_ref, dv_ref, gg_out_ref, wg_ref,
    k_all, v_all, q_all, do_all, u_ref, og_ref, w_ref, gh_blk, gh_own, gg, ends_own, ends_sib, att, slope,
    q_own, k_own, v_own, do_own, place_c, begin_c,
    stat, stat_in, cen_blk, cen_in, norm_own, dq_acc, dk_acc, dv_acc, out_blk,
    w_part, w_sib, w_sum, w_xa, w_ya, w_b, w_xb, w_yb, w_16, w_z, w_fin,
    l_sem, a_send, a_recv, y_send, y_recv, s_send, s_recv, e_sem, t_send, t_recv, n_send, n_recv, m_send, m_recv,
    f_send, f_recv, ws_sem, wx_send, wx_recv, wy_send, wy_recv, wz_send, wz_recv, wb_send, wb_recv,
):
    d = lax.axis_index("dp")
    s = lax.axis_index("seq")
    x, c = d // 2, d % 2
    z, y = s // YN, s % YN
    row, head = z // HEADS, z % HEADS
    core_of_z = ((z + 1) // 2) % 2
    slot_of_z = z // 2
    right, left, across = (y + 1) % YN, (y + 3) % YN, (y + 2) % YN

    def zmap(core, j):
        return 2 * j + core if j % 2 == 0 else 2 * j + 1 - core

    def at(core, zz, yy):
        return (2 * x + core, YN * zz + yy)

    sibling = at(1 - c, z, y)
    to_right, to_left = at(c, z, right), at(c, z, left)

    def remote(src, dst, send, recv, device):
        return pltpu.make_async_remote_copy(
            src_ref=src, dst_ref=dst, send_sem=send, recv_sem=recv,
            device_id=device, device_id_type=MESH,
        )

    def landed(dst, sem):
        pltpu.make_async_copy(dst, dst, sem).wait()

    home = [(at(core_of_z, HEADS * c + h, y), (core_of_z == c) & (HEADS * c + h == z)) for h in range(HEADS)]
    owner = [(at(row, zmap(c, j), y), (row == c) & (zmap(c, j) == z)) for j in range(SLOTS)]
    own_z = [zmap(c, j) for j in range(SLOTS)]
    collector = z == d

    bar = pltpu.get_barrier_semaphore()

    def greet(device):
        pl.semaphore_signal(bar, inc=1, device_id=device, device_id_type=MESH)

    for device, mine in home + owner:
        @pl.when(jnp.logical_not(mine))
        def _():
            greet(device)
    for h in range(HEADS):
        @pl.when(h != head)
        def _():
            greet(at(c, HEADS * row + h, y))

    @pl.when(collector)
    def _():
        for zz in range(ZN):
            @pl.when(zz != z)
            def _():
                greet((d, YN * zz + y))

    @pl.when(jnp.logical_not(collector))
    def _():
        greet((z, s))

    for step in range(1, YN):
        greet(at(c, z, (y + step) % YN))
        greet((2 * ((x + step) % 4) + c, s))
    greet(sibling)

    loads = [pltpu.make_async_copy(src, dst, l_sem.at[i]) for i, (src, dst) in enumerate(
        ((w_hbm, w_ref), (og_hbm, og_ref), (u_hbm, u_ref)))]
    for load in loads:
        load.start()
    total = jnp.zeros((1, 1), jnp.int32)
    ends_own[...] = jnp.zeros_like(ends_own)
    for h in range(3):
        total = total + len_ref[:, h:h + 1]
        ends_own[h:h + 1, :] = jnp.broadcast_to(total, (1, CHUNK))
    for load in loads:
        load.wait()
    gg[...] = dot(og_ref[...], w_ref[...], NT)
    gh_own[...] = (gg[...] * u_ref[...].astype(F32) * gain_ref[...]).astype(BF)

    selfs = (home[0][1] | home[1][1] | home[2][1] | home[3][1]).astype(jnp.int32)
    pl.semaphore_wait(bar, 8 - 2 * selfs + 3 + 3 + 1 + 3 + jnp.where(collector, ZN - 1, 1))

    block = (y, slot_of_z, core_of_z)

    def scatter(a, src, dst):
        for h in range(HEADS):
            device, mine = home[h]
            cols = src.at[:, h * HEAD:(h + 1) * HEAD]

            @pl.when(mine)
            def _():
                pltpu.make_async_copy(cols, dst, a_recv.at[a, slot_of_z]).start()

            @pl.when(jnp.logical_not(mine))
            def _():
                remote(cols, dst, a_send.at[a, h], a_recv.at[a, slot_of_z], device).start()

    def scattered(a):
        for h in range(HEADS):
            @pl.when(jnp.logical_not(home[h][1]))
            def _():
                sent(gh_blk.at[0], a_send.at[a, h])

    def sent(src, sem):
        pltpu.make_async_copy(src, src, sem).wait()

    gathered = (k_all, v_all, q_all, do_all)
    HALF = TOK // 2
    low, high = pl.ds(0, HALF), pl.ds(HALF, HALF)

    near = (y, left, right, across)

    def direct(a, j):
        ref = gathered[a].at[y, j, c]
        remote(ref, ref, y_send.at[a, j, 0], y_recv.at[a, j, 0], to_right).start()
        remote(ref, ref, y_send.at[a, j, 1], y_recv.at[a, j, 1], to_left).start()

    def forward(a, j):
        ref = gathered[a].at[left, j, c]
        landed(ref, y_recv.at[a, j, 0])
        half = ref.at[low]
        remote(half, half, y_send.at[a, j, 2], y_recv.at[a, j, 2], to_right).start()
        ref = gathered[a].at[right, j, c]
        landed(ref, y_recv.at[a, j, 1])
        half = ref.at[high]
        remote(half, half, y_send.at[a, j, 3], y_recv.at[a, j, 3], to_left).start()

    def share(a, n):
        if n == 3:
            for j in range(SLOTS):
                ref = gathered[a].at[across, j, c]
                landed(ref.at[low], y_recv.at[a, j, 2])
                landed(ref.at[high], y_recv.at[a, j, 3])
        ref = gathered[a].at[near[n], :, c]
        remote(ref, ref, s_send.at[a, n], s_recv.at[a, n], sibling).start()

    def shared(a, n):
        landed(gathered[a].at[near[n], :, 1 - c], s_recv.at[a, n])

    def start_of(place, ends):
        return jnp.where(place >= ends[2], ends[2], jnp.where(
            place >= ends[1], ends[1], jnp.where(place >= ends[0], ends[0], 0)))

    def near_at(g):
        return jnp.where(g == 0, y, jnp.where(g == 1, left, jnp.where(g == 2, right, across)))

    def pair_of(ref, yy, j):
        return ref[yy, j].reshape(PAIR, HEAD)

    def pair_place(yy, j, lanes):
        first, second = (YN * zmap(core, j) + yy for core in range(2))
        return jnp.where(lanes < TOK, first * TOK, (second - 1) * TOK) + lanes

    lanes = lax.broadcasted_iota(jnp.int32, (1, PAIR), 1)

    def attend(g):
        yy = near_at(g)
        for j in range(SLOTS):
            rows = (SLOTS - j) * TOK
            queries = q_own[j * TOK:, :]
            half = dot(queries, pair_of(k_all, yy, j), NT) * (0.5 * SCALE)
            key_place = pair_place(yy, j, lanes)
            visible = (key_place <= place_c[j * TOK:, :]) & (key_place >= begin_c[j * TOK:, :])
            plus = jnp.where(visible, 1.0 + jnp.tanh(half), 0.0)
            weights = half * plus
            slope[g, j, 0:rows] = plus + weights * (2.0 - plus)
            att[j * TOK:, :] += dot(weights.astype(BF), pair_of(v_all, yy, j))

    def attend_back(g, carry):
        yy = near_at(g)
        for j in range(SLOTS):
            rows = (SLOTS - j) * TOK
            gw = dot(do_own[j * TOK:, :], pair_of(v_all, yy, j), NT)
            dq_acc[j * TOK:, :] += dot((gw * slope[g, j, 0:rows]).astype(BF), pair_of(k_all, yy, j))
        return carry

    def key_back(g):
        yy = near_at(g)
        for j in reversed(range(SLOTS)):
            rows = (j + 1) * TOK
            queries, grads_out = pair_of(q_all, yy, j), pair_of(do_all, yy, j)
            half = dot(k_own[0:rows, :], queries, NT) * (0.5 * SCALE)
            gw = dot(v_own[0:rows, :], grads_out, NT)
            place = pair_place(yy, j, lanes)
            begin = start_of(place, [ends[h:h + 1, 0:PAIR] for h in range(3)])
            key_place = place_c[0:rows, :]
            visible = (key_place <= place) & (key_place >= begin)
            plus = jnp.where(visible, 1.0 + jnp.tanh(half), 0.0)
            weights = half * plus
            dv_acc[0:rows, :] += dot(weights.astype(BF), grads_out)
            dk_acc[0:rows, :] += dot((gw * (plus + weights * (2.0 - plus))).astype(BF), queries)

    remote(ends_own, ends_sib, e_sem.at[0], e_sem.at[1], sibling).start()
    scatter(0, k_ref, k_all.at[block])
    scattered(0)
    scatter(1, v_ref, v_all.at[block])
    for j in range(SLOTS):
        landed(k_all.at[y, j, c], a_recv.at[0, j])
        direct(0, j)
    share(0, 0)
    scattered(1)
    scatter(2, q_ref, q_all.at[block])
    for j in range(SLOTS):
        landed(v_all.at[y, j, c], a_recv.at[1, j])
        direct(1, j)
    share(1, 0)
    att[...] = jnp.zeros_like(att)
    landed(ends_sib, e_sem.at[1])
    ends = jnp.where(row == c, ends_own[...], ends_sib[...])
    for j in range(SLOTS):
        k_own[j * TOK:(j + 1) * TOK, :] = k_all[y, j, c]
        v_own[j * TOK:(j + 1) * TOK, :] = v_all[y, j, c]
        place = (YN * own_z[j] + y) * TOK + lax.broadcasted_iota(jnp.int32, (TOK, 1), 0)
        place_c[j * TOK:(j + 1) * TOK, :] = place
        begin_c[j * TOK:(j + 1) * TOK, :] = start_of(place, [ends[h:h + 1, 0:1] for h in range(3)])
    for j in range(SLOTS):
        forward(0, j)
    share(0, 1)
    share(0, 2)
    scattered(2)
    scatter(3, gh_own, gh_blk.at[slot_of_z])
    for j in range(SLOTS):
        landed(q_all.at[y, j, c], a_recv.at[2, j])
        q_own[j * TOK:(j + 1) * TOK, :] = q_all[y, j, c]

    def forward_step(g, carry):
        @pl.when(g == 0)
        def _():
            shared(0, 0)
            shared(1, 0)

        @pl.when(g == 1)
        def _():
            for j in range(SLOTS):
                forward(1, j)
            share(1, 1)
            share(1, 2)
            share(0, 3)
            for a in range(2):
                shared(a, 1)

        @pl.when(g == 2)
        def _():
            for a in range(2):
                shared(a, 2)

        @pl.when(g == 3)
        def _():
            share(1, 3)
            for j in range(SLOTS):
                direct(2, j)
            share(2, 0)
            for a in range(2):
                shared(a, 3)

        attend(g)
        return carry

    lax.fori_loop(0, 4, forward_step, 0)

    head_cols = pl.ds(pl.multiple_of(head * HEAD, HEAD), HEAD)

    def give_back(src, dst, send, recv, j):
        device, mine = owner[j]

        @pl.when(mine)
        def _():
            pltpu.make_async_copy(src, dst, recv).start()

        @pl.when(jnp.logical_not(mine))
        def _():
            remote(src, dst, send, recv, device).start()

    for j in range(SLOTS):
        landed(gh_blk.at[j], a_recv.at[3, j])
    lane = lax.broadcasted_iota(jnp.int32, (TOK, HEAD), 1)
    for j in range(SLOTS):
        block_gh = gh_blk[j].astype(F32)
        block_att = att[j * TOK:(j + 1) * TOK, :]
        head_mean = jnp.mean(block_att, axis=1, keepdims=True)
        centred = block_att - head_mean
        packed = jnp.where(lane == 0, head_mean, 0.0)
        packed = jnp.where(lane == 1, jnp.sum(centred * centred, axis=1, keepdims=True), packed)
        packed = jnp.where(lane == 2, jnp.sum(block_gh * centred, axis=1, keepdims=True), packed)
        packed = jnp.where(lane == 3, jnp.sum(block_gh, axis=1, keepdims=True), packed)
        stat[head, j] = jnp.transpose(packed)[0:8]
        cen_blk[j] = centred.astype(BF)
    for h in range(HEADS):
        @pl.when(h != head)
        def _():
            remote(stat.at[head], stat.at[head], t_send.at[h], t_recv.at[head],
                   at(c, HEADS * row + h, y)).start()
    for j in range(SLOTS):
        give_back(stat.at[head, j], stat_in.at[head], m_send.at[j], m_recv.at[head], j)
    for j in range(SLOTS):
        give_back(cen_blk.at[j], cen_in.at[:, head_cols], n_send.at[j], n_recv.at[head], j)
    dq_acc[...] = jnp.zeros_like(dq_acc)
    for j in range(SLOTS):
        forward(2, j)

    def combined(parts):
        means = [part[0:1] for part in parts]
        mean = (means[0] + means[1] + means[2] + means[3]) * (1.0 / HEADS)
        square, cross, grad_sum = 0.0, 0.0, 0.0
        for part in parts:
            off = part[0:1] - mean
            square += part[1:2] + HEAD * off * off
            cross += part[2:3] + off * part[3:4]
            grad_sum += part[3:4]
        inv_std = 1.0 / jnp.sqrt(square * (1.0 / QK) + EPS)
        return [mean, inv_std, grad_sum * (1.0 / QK), cross * inv_std * (1.0 / QK)] + means

    def columns(rows):
        pad = jnp.zeros((HEAD - len(rows), TOK), F32)
        cols = jnp.transpose(jnp.concatenate(rows + [pad], axis=0))
        return [cols[:, i:i + 1] for i in range(len(rows))]

    for h in range(HEADS):
        @pl.when(h != head)
        def _():
            landed(stat.at[h], t_recv.at[h])
    for j in reversed(range(SLOTS)):
        mean_c, inv_c, gmean_c, proj_c = columns(combined([stat[h, j] for h in range(HEADS)])[:4])
        unit = (att[j * TOK:(j + 1) * TOK, :] - mean_c) * inv_c
        attn_grad = (inv_c * (gh_blk[j].astype(F32) - gmean_c - unit * proj_c)).astype(BF)
        do_all[y, j, c] = attn_grad
        do_own[j * TOK:(j + 1) * TOK, :] = attn_grad
        direct(3, j)
    share(3, 0)
    share(2, 1)
    share(2, 2)

    def project():
        for h in range(HEADS):
            landed(cen_in.at[:, h * HEAD:(h + 1) * HEAD], n_recv.at[h])
            landed(stat_in.at[h], m_recv.at[h])
        cols = columns(combined([stat_in[h] for h in range(HEADS)]))
        normed = jnp.concatenate([
            cen_in[:, h * HEAD:(h + 1) * HEAD].astype(F32) + (cols[4 + h] - cols[0]) for h in range(HEADS)
        ], axis=1) * cols[1] * gain_ref[...]
        gated = (normed * u_ref[...].astype(F32)).astype(BF)
        w_part[...] = dot(jnp.transpose(gated), og_ref[...]).astype(BF).reshape(4, 2, 64, WIDTH)
        remote(w_part.at[:, 1 - c], w_sib, ws_sem.at[0], ws_sem.at[1], sibling).start()
        norm_own[...] = normed

    def project_out():
        normed = norm_own[...]
        gated = (normed * u_ref[...].astype(F32)).astype(BF)
        gg_out_ref[...] = (gg[...] * normed).astype(BF)
        lay_ref[...] = dot(gated, w_ref[...]).astype(BF)

    HW = WIDTH // 2
    first_half, second_half = pl.ds(0, HW), pl.ds(HW, HW)

    def weight_a():
        landed(w_sib, ws_sem.at[1])
        w_sum[...] = (w_part[:, c].astype(F32) + w_sib[...].astype(F32)).astype(BF).reshape(4, YN, 16, WIDTH)
        for n in range(3):
            to = (x + n + 1) % 4
            remote(w_sum.at[to, :, :, first_half], w_xa.at[n], wx_send.at[n], wx_recv.at[n],
                   (2 * to + c, s)).start()
            to = (y + n + 1) % YN
            remote(w_sum.at[:, to, :, second_half], w_ya.at[n], wy_send.at[n], wy_recv.at[n],
                   at(c, z, to)).start()

    def weight_b():
        for n in range(3):
            landed(w_xa.at[n], wx_recv.at[n])
            landed(w_ya.at[n], wy_recv.at[n])
        w_b[0] = (w_sum[x, :, :, 0:HW].astype(F32) + w_xa[0].astype(F32) + w_xa[1].astype(F32)
                  + w_xa[2].astype(F32)).astype(BF)
        w_b[1] = (w_sum[:, y, :, HW:].astype(F32) + w_ya[0].astype(F32) + w_ya[1].astype(F32)
                  + w_ya[2].astype(F32)).astype(BF)
        for n in range(3):
            to = (y + n + 1) % YN
            remote(w_b.at[0, to], w_yb.at[n], wy_send.at[n + 3], wy_recv.at[n + 3], at(c, z, to)).start()
            to = (x + n + 1) % 4
            remote(w_b.at[1, to], w_xb.at[n], wx_send.at[n + 3], wx_recv.at[n + 3], (2 * to + c, s)).start()

    def weight_z():
        for n in range(3):
            landed(w_yb.at[n], wy_recv.at[n + 3])
            landed(w_xb.at[n], wx_recv.at[n + 3])
        w_16[:, 0:HW] = (w_b[0, y].astype(F32) + w_yb[0].astype(F32) + w_yb[1].astype(F32)
                         + w_yb[2].astype(F32)).astype(BF)
        w_16[:, HW:] = (w_b[1, x].astype(F32) + w_xb[0].astype(F32) + w_xb[1].astype(F32)
                        + w_xb[2].astype(F32)).astype(BF)

        @pl.when(jnp.logical_not(collector))
        def _():
            remote(w_16, w_z.at[z], wz_send, wz_recv.at[z], (d, YN * d + y)).start()

    def weight_all():
        @pl.when(collector)
        def _():
            w_z[z] = w_16[...]
            for zz in range(ZN):
                @pl.when(zz != z)
                def _():
                    landed(w_z.at[zz], wz_recv.at[zz])
            total = w_z[0].astype(F32)
            for zz in range(1, ZN):
                total += w_z[zz].astype(F32)
            w_fin[...] = (total * (ALL_ROWS ** (-0.5))).astype(BF)
            for dd in range(8):
                @pl.when(dd != d)
                def _():
                    remote(w_fin, w_fin, wb_send.at[dd], wb_recv, (dd, s)).start()

    lax.fori_loop(0, 4, attend_back, 0)
    for j in reversed(range(SLOTS)):
        forward(3, j)
    share(3, 1)
    share(3, 2)
    out_blk[2] = (dq_acc[...] * (0.5 * SCALE)).astype(BF).reshape(SLOTS, TOK, HEAD)
    for j in range(SLOTS):
        give_back(out_blk.at[2, j], dq_ref.at[:, head_cols], f_send.at[2, j], f_recv.at[2, head], j)
    project()
    dk_acc[...] = jnp.zeros_like(dk_acc)
    dv_acc[...] = jnp.zeros_like(dv_acc)

    def backward_step(g, carry):
        for n in range(4):
            @pl.when(g == n)
            def _():
                if n == 2:
                    weight_a()
                if n == 3:
                    share(2, 3)
                    share(3, 3)
                for a in (2, 3):
                    shared(a, n)

        key_back(g)
        return carry

    lax.fori_loop(0, 4, backward_step, 0)
    out_blk[0] = (dk_acc[...] * (0.5 * SCALE)).astype(BF).reshape(SLOTS, TOK, HEAD)
    for j in range(SLOTS):
        give_back(out_blk.at[0, j], dk_ref.at[:, head_cols], f_send.at[0, j], f_recv.at[0, head], j)
    out_blk[1] = dv_acc[...].astype(BF).reshape(SLOTS, TOK, HEAD)
    for j in range(SLOTS):
        give_back(out_blk.at[1, j], dv_ref.at[:, head_cols], f_send.at[1, j], f_recv.at[1, head], j)
    weight_b()
    weight_z()
    project_out()
    weight_all()

    @pl.when(collector)
    def _():
        for dd in range(8):
            @pl.when(dd != d)
            def _():
                sent(w_fin, wb_send.at[dd])

    @pl.when(jnp.logical_not(collector))
    def _():
        landed(w_fin, wb_recv)
        sent(w_16, wz_send)

    wg_ref[...] = w_fin[...].astype(F32)
    for a, dst in ((0, dk_ref), (1, dv_ref), (2, dq_ref)):
        for h in range(HEADS):
            landed(dst.at[:, h * HEAD:(h + 1) * HEAD], f_recv.at[a, h])
    sent(ends_own, e_sem.at[0])
    sent(w_sib, ws_sem.at[0])
    scattered(3)
    for h in range(HEADS):
        @pl.when(h != head)
        def _():
            sent(stat.at[head], t_send.at[h])
    for j in range(SLOTS):
        @pl.when(jnp.logical_not(owner[j][1]))
        def _():
            sent(cen_blk.at[j], n_send.at[j])
            sent(stat_in.at[0], m_send.at[j])
            for a in range(3):
                sent(out_blk.at[a, j], f_send.at[a, j])
        for a in range(4):
            for n in range(2):
                sent(gh_blk.at[0], y_send.at[a, j, n])
                sent(gh_blk.at[0, low], y_send.at[a, j, n + 2])
            sent(k_all.at[0, :, 0], s_send.at[a, j])
    for n in range(3):
        sent(w_xa.at[n], wx_send.at[n])
        sent(w_ya.at[n], wy_send.at[n])
        sent(w_xb.at[n], wx_send.at[n + 3])
        sent(w_yb.at[n], wy_send.at[n + 3])


def copy_kernel(*refs):
    count = len(refs) // 2
    for source, result in zip(refs[:count], refs[count:]):
        result[...] = source[...]


def per_device(queries, keys, values, gates, gain, out_weight, out_grad, lengths):
    vm = pl.BlockSpec(memory_space=pltpu.VMEM)
    anywhere = pl.BlockSpec(memory_space=pl.ANY)
    block = (SLOTS, TOK, HEAD)
    whole = (YN, SLOTS, 2, TOK, HEAD)
    own = (CHUNK, HEAD)
    dma = pltpu.SemaphoreType.DMA
    scratch = [
        pltpu.VMEM(whole, BF),
        pltpu.VMEM(whole, BF),
        pltpu.VMEM(whole, BF),
        pltpu.VMEM(whole, BF),
        pltpu.VMEM((TOK, QK), BF),
        pltpu.VMEM((TOK, WIDTH), BF),
        pltpu.VMEM((QK, WIDTH), BF),
        pltpu.VMEM(block, BF),
        pltpu.VMEM((TOK, QK), BF),
        pltpu.VMEM((TOK, QK), F32),
        pltpu.VMEM((8, CHUNK), jnp.int32),
        pltpu.VMEM((8, CHUNK), jnp.int32),
        pltpu.VMEM(own, F32),
        pltpu.VMEM((YN, SLOTS, CHUNK, PAIR), F32),
        pltpu.VMEM(own, BF),
        pltpu.VMEM(own, BF),
        pltpu.VMEM(own, BF),
        pltpu.VMEM(own, BF),
        pltpu.VMEM((CHUNK, 1), jnp.int32),
        pltpu.VMEM((CHUNK, 1), jnp.int32),
        pltpu.VMEM((HEADS, SLOTS, 8, TOK), F32),
        pltpu.VMEM((HEADS, 8, TOK), F32),
        pltpu.VMEM(block, BF),
        pltpu.VMEM((TOK, QK), BF),
        pltpu.VMEM((TOK, QK), F32),
        pltpu.VMEM(own, F32),
        pltpu.VMEM(own, F32),
        pltpu.VMEM(own, F32),
        pltpu.VMEM((3, SLOTS, TOK, HEAD), BF),
        pltpu.VMEM((4, 2, 64, WIDTH), BF),
        pltpu.VMEM((4, 64, WIDTH), BF),
        pltpu.VMEM((4, YN, 16, WIDTH), BF),
        pltpu.VMEM((3, YN, 16, WIDTH // 2), BF),
        pltpu.VMEM((3, YN, 16, WIDTH // 2), BF),
        pltpu.VMEM((2, YN, 16, WIDTH // 2), BF),
        pltpu.VMEM((3, 16, WIDTH // 2), BF),
        pltpu.VMEM((3, 16, WIDTH // 2), BF),
        pltpu.VMEM((16, WIDTH), BF),
        pltpu.VMEM((ZN, 16, WIDTH), BF),
        pltpu.VMEM((16, WIDTH), BF),
        dma((3,)),
        dma((4, 4)), dma((4, 4)),
        dma((4, 4, 4)), dma((4, 4, 4)),
        dma((4, 4)), dma((4, 4)),
        dma((2,)),
        dma((4,)), dma((4,)),
        dma((4,)), dma((4,)),
        dma((4,)), dma((4,)),
        dma((3, 4)), dma((3, 4)),
        dma((2,)),
        dma((6,)), dma((6,)),
        dma((6,)), dma((6,)),
        dma, dma((8,)),
        dma((8,)), dma,
    ]
    shapes = (
        jax.ShapeDtypeStruct((TOK, WIDTH), BF),
        jax.ShapeDtypeStruct((TOK, QK), BF),
        jax.ShapeDtypeStruct((TOK, QK), BF),
        jax.ShapeDtypeStruct((TOK, QK), BF),
        jax.ShapeDtypeStruct((TOK, QK), BF),
        jax.ShapeDtypeStruct((16, WIDTH), F32),
    )
    results = pl.pallas_call(
        layer_kernel,
        out_shape=shapes,
        in_specs=[anywhere] * 6 + [vm] * 2,
        out_specs=(vm,) * 6,
        scratch_shapes=scratch,
        compiler_params=pltpu.CompilerParams(
            collective_id=0, has_side_effects=True, vmem_limit_bytes=56 * 1024 * 1024
        ),
    )(
        queries, keys, values, gates, out_grad, out_weight,
        gain.reshape(1, QK), lengths,
    )
    return pl.pallas_call(
        copy_kernel,
        out_shape=shapes,
        in_specs=[vm] * 6,
        out_specs=(vm,) * 6,
    )(*results)


def solution(mesh):
    rows = P(("dp", "seq"), None)

    def program(queries, keys, values, gates, gain, out_weight, out_grad, lengths):
        return jax.shard_map(
            per_device,
            mesh=mesh,
            in_specs=(rows, rows, rows, rows, P(), P(), rows, P("dp", None)),
            out_specs=(rows, rows, rows, rows, rows, P("seq", None)),
            check_vma=False,
        )(queries, keys, values, gates, gain, out_weight, out_grad, lengths)

    return program
```

time: 105 us -> 86 us (0.82); the launches traced: 105 us -> 84.4 us
  Pallas kernels: 96.4 us -> 83.8 us
  local copies, waits for them, and re-layouts: 7.62 us -> 0 us
    pallas_call x1 -> x2, Pallas kernels: 96.4 us -> 83.8 us  [the longest x1 81.4 us: per_device(): pl.pallas_call(layer_kernel, out_shape=shapes, in_specs=[anywhere] * 6 +...]
    unnamed x18 -> x0, local copies, waits for them, and re-layouts: 6.94 us -> none
where the time goes in v2:
time: 86 us; the launch traced here: 84.4 us
  Pallas kernels  83.8 us (97%)
    pallas_call x1, Pallas kernels, per_device(): pl.pallas_call(layer_kernel, out_shape=shapes, in_specs=[anywhere] * 6 +...  81.4 us
    pallas_call x1, Pallas kernels, per_device(): pl.pallas_call(copy_kernel, out_shape=shapes, in_specs=[vm] * 6, out_spec...  2.34 us

profile of v2, /device:TPU:1, one launch (start us, length us, event | category | flops | bytes accessed | tf_op | source)
XLA Modules:
  0.0 84.4 jit_solution(8294089687645490760)
XLA Ops:
  0.6 81.4 %shard_map.127 = (bf16[192,1024]{1,0:T(8,128)(2,1)}, bf16[192,512]{1,0:T(8,128)(2,1)}, bf16[192,512]{1,0:T(8,128)(2,1)}, bf16[192,512]{1,0:T(8,128)(2,1)}, bf16[192,512]{1,0:T(8,128)(2,1)}, /*index=5*/f32[16,1024]{1,0:T(8,128)}) custom-call(bf16[192,512]{1,0:T(8,128)(2,1)} %q_ref.1, bf16[192,512]{1,0:T(8,128)(2,1)} %k_ref.1, bf16[192,512]{1,0:T(8,128)(2,1)} %v_ref.1, ...), custom_call_target="tpu_custom_call" | custom-call | tf_op jit(solution)/shard_map/pallas_call | solution.py:606
  82.1 2.3 %shard_map.128 = (bf16[192,1024]{1,0:T(8,128)(2,1)}, bf16[192,512]{1,0:T(8,128)(2,1)}, bf16[192,512]{1,0:T(8,128)(2,1)}, bf16[192,512]{1,0:T(8,128)(2,1)}, bf16[192,512]{1,0:T(8,128)(2,1)}, /*index=5*/f32[16,1024]{1,0:T(8,128)}) custom-call(bf16[192,1024]{1,0:T(8,128)(2,1)} %get-tuple-element.12.refs_0_, bf16[192,512]{1,0:T(8,128)(2,1)} %get-tuple-element.13.refs_1_, ...), custom_call_target="tpu_custom_call" | custom-call | tf_op jit(solution)/shard_map/pallas_call | solution.py:619

commit v3 on v2

--- a/solution.py
+++ b/solution.py
@@ -206,6 +206,18 @@
 
     def attend_back(g, carry):
         yy = near_at(g)
+
+        @pl.when(g == 2)
+        def _():
+            project()
+
+        @pl.when(g == 3)
+        def _():
+            for j in reversed(range(SLOTS)):
+                forward(3, j)
+            share(3, 1)
+            share(3, 2)
+
         for j in range(SLOTS):
             rows = (SLOTS - j) * TOK
             gw = dot(do_own[j * TOK:, :], pair_of(v_all, yy, j), NT)
@@ -446,14 +458,10 @@
                     remote(w_fin, w_fin, wb_send.at[dd], wb_recv, (dd, s)).start()
 
     lax.fori_loop(0, 4, attend_back, 0)
-    for j in reversed(range(SLOTS)):
-        forward(3, j)
-    share(3, 1)
-    share(3, 2)
     out_blk[2] = (dq_acc[...] * (0.5 * SCALE)).astype(BF).reshape(SLOTS, TOK, HEAD)
     for j in range(SLOTS):
         give_back(out_blk.at[2, j], dq_ref.at[:, head_cols], f_send.at[2, j], f_recv.at[2, head], j)
-    project()
+    weight_a()
     dk_acc[...] = jnp.zeros_like(dk_acc)
     dv_acc[...] = jnp.zeros_like(dv_acc)
 
@@ -462,10 +470,9 @@
             @pl.when(g == n)
             def _():
                 if n == 2:
-                    weight_a()
-                if n == 3:
                     share(2, 3)
                     share(3, 3)
+                    weight_b()
                 for a in (2, 3):
                     shared(a, n)
 
@@ -473,14 +480,13 @@
         return carry
 
     lax.fori_loop(0, 4, backward_step, 0)
+    weight_z()
     out_blk[0] = (dk_acc[...] * (0.5 * SCALE)).astype(BF).reshape(SLOTS, TOK, HEAD)
     for j in range(SLOTS):
         give_back(out_blk.at[0, j], dk_ref.at[:, head_cols], f_send.at[0, j], f_recv.at[0, head], j)
     out_blk[1] = dv_acc[...].astype(BF).reshape(SLOTS, TOK, HEAD)
     for j in range(SLOTS):
         give_back(out_blk.at[1, j], dv_ref.at[:, head_cols], f_send.at[1, j], f_recv.at[1, head], j)
-    weight_b()
-    weight_z()
     project_out()
     weight_all()
 

time: 86 us -> 82.6 us (0.960); the launches traced: 84.4 us -> 82.4 us
  Pallas kernels: 83.8 us -> 81.8 us
    pallas_call x1, Pallas kernels: 81.4 us -> 79.4 us  [per_device(): pl.pallas_call(layer_kernel, out_shape=shapes, in_specs=[anywhere] * 6 +...]
where the time goes in v3:
time: 82.6 us; the launch traced here: 82.4 us
  Pallas kernels  81.8 us (99%)
    pallas_call x1, Pallas kernels, per_device(): pl.pallas_call(layer_kernel, out_shape=shapes, in_specs=[anywhere] * 6 +...  79.4 us
    pallas_call x1, Pallas kernels, per_device(): pl.pallas_call(copy_kernel, out_shape=shapes, in_specs=[vm] * 6, out_spec...  2.34 us

profile of v3, /device:TPU:1, one launch (start us, length us, event | category | flops | bytes accessed | tf_op | source)
XLA Modules:
  0.0 82.4 jit_solution(11040029171646877094)
XLA Ops:
  0.6 79.4 %shard_map.127 = (bf16[192,1024]{1,0:T(8,128)(2,1)}, bf16[192,512]{1,0:T(8,128)(2,1)}, bf16[192,512]{1,0:T(8,128)(2,1)}, bf16[192,512]{1,0:T(8,128)(2,1)}, bf16[192,512]{1,0:T(8,128)(2,1)}, /*index=5*/f32[16,1024]{1,0:T(8,128)}) custom-call(bf16[192,512]{1,0:T(8,128)(2,1)} %q_ref.1, bf16[192,512]{1,0:T(8,128)(2,1)} %k_ref.1, bf16[192,512]{1,0:T(8,128)(2,1)} %v_ref.1, ...), custom_call_target="tpu_custom_call" | custom-call | tf_op jit(solution)/shard_map/pallas_call | solution.py:612
  80.1 2.3 %shard_map.128 = (bf16[192,1024]{1,0:T(8,128)(2,1)}, bf16[192,512]{1,0:T(8,128)(2,1)}, bf16[192,512]{1,0:T(8,128)(2,1)}, bf16[192,512]{1,0:T(8,128)(2,1)}, bf16[192,512]{1,0:T(8,128)(2,1)}, /*index=5*/f32[16,1024]{1,0:T(8,128)}) custom-call(bf16[192,1024]{1,0:T(8,128)(2,1)} %get-tuple-element.12.refs_0_, bf16[192,512]{1,0:T(8,128)(2,1)} %get-tuple-element.13.refs_1_, ...), custom_call_target="tpu_custom_call" | custom-call | tf_op jit(solution)/shard_map/pallas_call | solution.py:625

commit v4 on v3

--- a/solution.py
+++ b/solution.py
@@ -196,12 +196,12 @@
         for j in range(SLOTS):
             rows = (SLOTS - j) * TOK
             queries = q_own[j * TOK:, :]
-            half = dot(queries, pair_of(k_all, yy, j), NT) * (0.5 * SCALE)
+            score = dot(queries, pair_of(k_all, yy, j), NT) * SCALE
             key_place = pair_place(yy, j, lanes)
             visible = (key_place <= place_c[j * TOK:, :]) & (key_place >= begin_c[j * TOK:, :])
-            plus = jnp.where(visible, 1.0 + jnp.tanh(half), 0.0)
-            weights = half * plus
-            slope[g, j, 0:rows] = plus + weights * (2.0 - plus)
+            gate = jnp.where(visible, jax.nn.sigmoid(score), 0.0)
+            weights = score * gate
+            slope[g, j, 0:rows] = gate + weights * (1.0 - gate)
             att[j * TOK:, :] += dot(weights.astype(BF), pair_of(v_all, yy, j))
 
     def attend_back(g, carry):
@@ -229,16 +229,16 @@
         for j in reversed(range(SLOTS)):
             rows = (j + 1) * TOK
             queries, grads_out = pair_of(q_all, yy, j), pair_of(do_all, yy, j)
-            half = dot(k_own[0:rows, :], queries, NT) * (0.5 * SCALE)
+            score = dot(k_own[0:rows, :], queries, NT) * SCALE
             gw = dot(v_own[0:rows, :], grads_out, NT)
             place = pair_place(yy, j, lanes)
             begin = start_of(place, [ends[h:h + 1, 0:PAIR] for h in range(3)])
             key_place = place_c[0:rows, :]
             visible = (key_place <= place) & (key_place >= begin)
-            plus = jnp.where(visible, 1.0 + jnp.tanh(half), 0.0)
-            weights = half * plus
+            gate = jnp.where(visible, jax.nn.sigmoid(score), 0.0)
+            weights = score * gate
             dv_acc[0:rows, :] += dot(weights.astype(BF), grads_out)
-            dk_acc[0:rows, :] += dot((gw * (plus + weights * (2.0 - plus))).astype(BF), queries)
+            dk_acc[0:rows, :] += dot((gw * (gate + weights * (1.0 - gate))).astype(BF), queries)
 
     remote(ends_own, ends_sib, e_sem.at[0], e_sem.at[1], sibling).start()
     scatter(0, k_ref, k_all.at[block])
@@ -458,7 +458,7 @@
                     remote(w_fin, w_fin, wb_send.at[dd], wb_recv, (dd, s)).start()
 
     lax.fori_loop(0, 4, attend_back, 0)
-    out_blk[2] = (dq_acc[...] * (0.5 * SCALE)).astype(BF).reshape(SLOTS, TOK, HEAD)
+    out_blk[2] = (dq_acc[...] * SCALE).astype(BF).reshape(SLOTS, TOK, HEAD)
     for j in range(SLOTS):
         give_back(out_blk.at[2, j], dq_ref.at[:, head_cols], f_send.at[2, j], f_recv.at[2, head], j)
     weight_a()
@@ -481,7 +481,7 @@
 
     lax.fori_loop(0, 4, backward_step, 0)
     weight_z()
-    out_blk[0] = (dk_acc[...] * (0.5 * SCALE)).astype(BF).reshape(SLOTS, TOK, HEAD)
+    out_blk[0] = (dk_acc[...] * SCALE).astype(BF).reshape(SLOTS, TOK, HEAD)
     for j in range(SLOTS):
         give_back(out_blk.at[0, j], dk_ref.at[:, head_cols], f_send.at[0, j], f_recv.at[0, head], j)
     out_blk[1] = dv_acc[...].astype(BF).reshape(SLOTS, TOK, HEAD)

time: 82.6 us -> 82.6 us (level)
  no operation moved by 1% of the time
where the time goes in v4:
time: 82.6 us; the launch traced here: 82.4 us
  Pallas kernels  81.8 us (99%)
    pallas_call x1, Pallas kernels, per_device(): pl.pallas_call(layer_kernel, out_shape=shapes, in_specs=[anywhere] * 6 +...  79.4 us
    pallas_call x1, Pallas kernels, per_device(): pl.pallas_call(copy_kernel, out_shape=shapes, in_specs=[vm] * 6, out_spec...  2.34 us

profile of v4, /device:TPU:1, one launch (start us, length us, event | category | flops | bytes accessed | tf_op | source)
XLA Modules:
  0.0 82.4 jit_solution(897133209638165260)
XLA Ops:
  0.6 79.4 %shard_map.127 = (bf16[192,1024]{1,0:T(8,128)(2,1)}, bf16[192,512]{1,0:T(8,128)(2,1)}, bf16[192,512]{1,0:T(8,128)(2,1)}, bf16[192,512]{1,0:T(8,128)(2,1)}, bf16[192,512]{1,0:T(8,128)(2,1)}, /*index=5*/f32[16,1024]{1,0:T(8,128)}) custom-call(bf16[192,512]{1,0:T(8,128)(2,1)} %q_ref.1, bf16[192,512]{1,0:T(8,128)(2,1)} %k_ref.1, bf16[192,512]{1,0:T(8,128)(2,1)} %v_ref.1, ...), custom_call_target="tpu_custom_call" | custom-call | tf_op jit(solution)/shard_map/pallas_call | solution.py:612
  80.1 2.3 %shard_map.128 = (bf16[192,1024]{1,0:T(8,128)(2,1)}, bf16[192,512]{1,0:T(8,128)(2,1)}, bf16[192,512]{1,0:T(8,128)(2,1)}, bf16[192,512]{1,0:T(8,128)(2,1)}, bf16[192,512]{1,0:T(8,128)(2,1)}, /*index=5*/f32[16,1024]{1,0:T(8,128)}) custom-call(bf16[192,1024]{1,0:T(8,128)(2,1)} %get-tuple-element.12.refs_0_, bf16[192,512]{1,0:T(8,128)(2,1)} %get-tuple-element.13.refs_1_, ...), custom_call_target="tpu_custom_call" | custom-call | tf_op jit(solution)/shard_map/pallas_call | solution.py:625
